TPU v7x, 32 devices: a whole 2x2x4 slice. The times are simulated.
32 devices in a mesh: groups: 2 (over x), ctx: 16 (over z, y, core).
Axes of the slice: x: 2, y: 2, z: 4, core: 2. Of those that a mesh axis runs over, the one named last changes fastest.
Arguments:
- hidden: bfloat16 [24576, 4096], P(('groups', 'ctx')), parts along dimension 0, may hold values from -6 to 6
- w_qkv: bfloat16 [4096, 768], P('ctx'), may hold values from -0.09375 to 0.09375
- w_out: bfloat16 [256, 4096], P('ctx'), may hold values from -0.375 to 0.375
- norm_gain: float32 [256], replicated, may hold values from 0.1 to 1.9
- incoming: float32 [4, 128, 128], P('groups'), parts along dimension 0, may hold values from -600 to 600
Outputs:
- attn_out: bfloat16 [24576, 4096], P(('groups', 'ctx')), parts along dimension 0
There are 2 independent parts, one for each index of `groups`. A program takes and returns all parts, laid end to end along the dimension named above; an argument that names none is the same for every part. Nothing has to cross between parts.
All inputs are finite; a program needn't handle non-finite values.
Results may differ from a plain program's by a relative error of at most 0.0065.
Values may be sent and summed in bfloat16 or wider, within the bound.
A program may use at most 64 MiB of HBM per device.

v0:
```python
import jax
import jax.numpy as jnp
from jax import lax
from jax.sharding import PartitionSpec as P


def carried_in(value, axis, join, neutral):
    count, mine = (lax.axis_size(axis), lax.axis_index(axis))
    pieces = lax.all_gather(value, axis)
    running = jnp.full_like(value, 0) + jnp.asarray(neutral, value.dtype)

    def turn(position, running):
        longer = join(running, pieces[position])
        return jnp.where(position < mine, longer, running)

    return lax.fori_loop(0, count - 1, turn, running)


def local(hidden, w_qkv, w_out, norm_gain, incoming):
    tokens_here = hidden.shape[0]
    width = w_qkv.shape[1] // 3
    heads = incoming.shape[0]
    head_size = incoming.shape[1]
    columns = hidden
    proj = jnp.dot(
        columns,
        lax.all_gather(w_qkv, "ctx", axis=0, tiled=True),
        preferred_element_type=jnp.float32,
    ).astype(jnp.bfloat16)
    query = proj[:, :width].reshape(tokens_here, heads, head_size)
    keys = proj[:, width : 2 * width].reshape(tokens_here, heads, head_size)
    values = proj[:, 2 * width :].reshape(tokens_here, heads, head_size)
    state = jnp.einsum("thd,the->hde", keys, values, preferred_element_type=jnp.float32)
    zero_state = jnp.zeros_like(state)

    def add_states(earlier, later):
        return earlier + later

    before = carried_in(state, "ctx", add_states, zero_state)
    prior = incoming + before
    scores = jnp.einsum("thd,shd->hts", query, keys, preferred_element_type=jnp.float32)
    rows = jnp.arange(tokens_here)
    causal = rows[:, None] >= rows[None, :]
    scores = jnp.where(causal[None], scores, 0.0).astype(jnp.bfloat16)
    intra = jnp.einsum("hts,she->the", scores, values, preferred_element_type=jnp.float32)
    cross = jnp.einsum(
        "thd,hde->the", query.astype(jnp.float32), prior, precision=lax.Precision.HIGHEST
    )
    mixed = intra + cross
    scale = lax.rsqrt(jnp.mean(mixed * mixed, axis=-1, keepdims=True) + 1e-06)
    gains = norm_gain.reshape(heads, head_size)
    normed = (mixed * scale * gains).astype(jnp.bfloat16).reshape(tokens_here, width)
    columns = normed
    result = jnp.dot(
        columns,
        lax.all_gather(w_out, "ctx", axis=0, tiled=True),
        preferred_element_type=jnp.float32,
    )
    return result.astype(jnp.bfloat16)


def solution(mesh):
    return jax.shard_map(
        local,
        mesh=mesh,
        in_specs=(
            P(("groups", "ctx"), None),
            P("ctx", None),
            P("ctx", None),
            P(),
            P("groups", None, None),
        ),
        out_specs=P(("groups", "ctx"), None),
        check_vma=False,
    )
```

profile of v0, /device:TPU:0, one launch (start us, length us, event | category | flops | bytes accessed | tf_op | source)
XLA Modules:
  0.0 179.5 jit_solution(12376154910145856354)
XLA Ops:
  6.5 0.0 all-gather.5.cloned.1.call-start
  6.5 0.7 all-gather.5.cloned.1.call-update
  7.3 0.0 all-gather.9.cloned.1.call-start
  7.3 66.9 %all-gather.5.cloned.1.call-done = bf16[4096,768]{1,0:T(8,128)(2,1)} async-done(((bf16[256,768]{1,0:T(8,128)(2,1)}), bf16[4096,768]{1,0:T(8,128)(2,1)}) %all-gather.5.cloned.1.call-update) | async-done | bytes 6291472 | tf_op jit(solution)/shard_map/all_gather | solution.py:27
  74.2 9.1 %convolution_convert_fusion.1 = bf16[768,768]{0,1:T(8,128)(2,1)S(1)} fusion(bf16[768,4096]{1,0:T(8,128)(2,1)} %param.7, bf16[4096,768]{1,0:T(8,128)(2,1)} %all-gather.5.cloned.1.call-done), kind=kOutput, calls=%fused_computation.8 | convolution fusion | flops 4832428032 | bytes 13762560 | tf_op jit(solution)/shard_map/dot_general | solution.py:25
  83.3 0.1 fusion.10
  83.4 0.0 copy-start
  83.4 0.9 fusion.11
  84.3 0.0 all-gather.9.cloned.1.call-update
  84.3 0.0 all-gather.7.cloned.1.call-start
  84.4 0.7 all-gather.7.cloned.1.call-update
  85.1 0.2 iota_compare_fusion
  85.3 39.2 %all-gather.9.cloned.1.call-done = f32[32,128,128]{2,1,0:T(8,128)} async-done(((f32[2,128,128]{2,1,0:T(8,128)}), f32[32,128,128]{2,1,0:T(8,128)}) %all-gather.9.cloned.1.call-update) | async-done | bytes 2097168 | tf_op jit(solution)/shard_map/all_gather | solution.py:9
  124.5 14.6 %while.14 = (s32[]{:T(128)}, f32[2,128,128]{2,1,0:T(8,128)S(1)}, s32[]{:T(128)}, f32[16,2,128,128]{3,2,1,0:T(8,128)}, s32[]{:T(128)}, /*index=5*/s32[]{:T(128)}) while((s32[]{:T(128)}, f32[2,128,128]{2,1,0:T(8,128)S(1)}, s32[]{:T(128)}, f32[16,2,128,128]{3,2,1,0:T(8,128)}, s32[]{:T(128)}, /*index=5*/s32[]{:T(128)}) %tuple.44), condition=%wide.region_1.2_spmd.clone, body=%wide.region_0.1_spmd.clone.sunk | while | flops 98308 | bytes 393317 | solution.py:16
  124.5 0.9 add_select_fusion.2
  125.5 0.9 add_select_fusion.2
  126.4 0.9 add_select_fusion.2
  127.4 0.9 add_select_fusion.2
  128.4 0.9 add_select_fusion.2
  129.4 0.9 add_select_fusion.2
  130.3 0.9 add_select_fusion.2
  131.3 0.9 add_select_fusion.2
  132.3 1.0 add_select_fusion.2
  133.3 1.0 add_select_fusion.2
  134.2 0.9 add_select_fusion.2
  135.2 0.9 add_select_fusion.2
  136.2 0.9 add_select_fusion.2
  137.2 0.9 add_select_fusion.2
  138.1 1.0 add_select_fusion.2
  139.1 0.0 copy-done
  139.1 0.5 fusion.7
  139.6 0.0 copy-start.1
  139.7 1.6 multiply_reduce_fusion
  141.3 0.0 copy-done.1
  141.3 0.1 multiply_convert_fusion
  141.4 25.4 %all-gather.7.cloned.1.call-done = bf16[256,4096]{1,0:T(8,128)(2,1)} async-done(((bf16[16,4096]{1,0:T(8,128)(2,1)}), bf16[256,4096]{1,0:T(8,128)(2,1)}) %all-gather.7.cloned.1.call-update) | async-done | bytes 2097168 | tf_op jit(solution)/shard_map/all_gather | solution.py:56
  166.8 6.1 %convolution_convert_fusion = bf16[768,4096]{1,0:T(8,128)(2,1)} fusion(bf16[768,256]{0,1:T(8,128)(2,1)S(1)} %bitcast.22, bf16[256,4096]{1,0:T(8,128)(2,1)} %all-gather.7.cloned.1.call-done), kind=kOutput, calls=%fused_computation.1 | convolution fusion | flops 1613758464 | bytes 8781824 | tf_op jit(solution)/shard_map/dot_general | solution.py:54
  (2 shorter events, 0.0 us)
Async XLA Ops:
  6.5 67.7 %all-gather.5.cloned.1.call-start = ((), (), s32[]{:S(2)}) async-start(), calls=%async_computation | async-start | bytes 6684672 | tf_op jit(solution)/shard_map/all_gather | solution.py:27
  7.3 117.2 %all-gather.9.cloned.1.call-start = ((), (), s32[]{:S(2)}) async-start(), calls=%async_computation.2 | async-start | bytes 2228224 | tf_op jit(solution)/shard_map/all_gather | solution.py:9
  83.4 55.7 %copy-start = (f32[2,128,128]{2,1,0:T(8,128)S(1)}, f32[2,128,128]{2,1,0:T(8,128)}, u32[]{:S(2)}) copy-start(f32[2,128,128]{2,1,0:T(8,128)} %param.11) | copy-start | bytes 393220
  84.3 82.5 %all-gather.7.cloned.1.call-start = ((), (), s32[]{:S(2)}) async-start(), calls=%async_computation.1 | async-start | bytes 2228224 | tf_op jit(solution)/shard_map/all_gather | solution.py:56
  139.6 1.7 copy-start.1
Sparse Core Ops, SparseCore 0:
  9.6 64.5 all-gather.4
  84.5 39.9 all-gather.8
  126.7 40.0 all-gather.6
where the time goes:
time: 180 us; the launch traced here: 179 us
  waiting for transfers between devices  133 us (74%)
  matrix products  18.3 us (10%)
  other arithmetic  14.6 us (8%)
  between operations  13.2 us (7%)
    all_gather x1, waiting for transfers between devices, local(): lax.all_gather(w_qkv, 'ctx', axis=0, tiled=True)  66.9 us
    all_gather x1, waiting for transfers between devices, carried_in(): pieces = lax.all_gather(value, axis)  39.2 us
    all_gather x1, waiting for transfers between devices, local(): lax.all_gather(w_out, 'ctx', axis=0, tiled=True)  25.4 us
    select_n x15, other arithmetic, turn(): return jnp.where(position < mine, longer, running)  14.3 us
    dot_general x1, matrix products, local(): jnp.dot(columns, lax.all_gather(w_qkv, 'ctx', axis=0, tiled=True), prefer...  9.06 us
    dot_general x1, matrix products, local(): jnp.dot(columns, lax.all_gather(w_out, 'ctx', axis=0, tiled=True), prefer...  6.12 us
  transfers between devices with their start and end apart: 3, of which 3 were waited for; matrix products, arithmetic and copies ran while one was open for 9% of the time, Pallas kernels for 0%

commit v1 on v0

--- a/solution.py
+++ b/solution.py
@@ -2,6 +2,31 @@
 import jax.numpy as jnp
 from jax import lax
 from jax.sharding import PartitionSpec as P
+
+
+def _review_core(frame):
+    seen_now = lax.axis_index("ctx")
+    n_now = lax.axis_size("ctx")
+    g_now, now, block_out = (n_now, seen_now, frame.shape[0])
+    z_new = tuple((t * g_now if rr == 0 else t for rr, t in enumerate(frame.shape)))
+    front = jnp.zeros(z_new, frame.dtype)
+    next_value = clean = frame
+    local_now = lax.dynamic_update_slice_in_dim(front, frame, now * block_out, axis=0)
+    ii = 1
+    while ii < g_now // 2 + 1:
+        vec_out = tuple(((rr, (rr + 1) % g_now) for rr in range(g_now)))
+        next_value = lax.ppermute(next_value, "ctx", vec_out)
+        local_now = lax.dynamic_update_slice_in_dim(
+            local_now, next_value, (now - ii) % g_now * block_out, axis=0
+        )
+        if 2 * ii < g_now:
+            met_up = tuple(((rr, (rr - 1) % g_now) for rr in range(g_now)))
+            clean = lax.ppermute(clean, "ctx", met_up)
+            local_now = lax.dynamic_update_slice_in_dim(
+                local_now, clean, (now + ii) % g_now * block_out, axis=0
+            )
+        ii += 1
+    return local_now
 
 
 def carried_in(value, axis, join, neutral):
@@ -51,11 +76,7 @@
     gains = norm_gain.reshape(heads, head_size)
     normed = (mixed * scale * gains).astype(jnp.bfloat16).reshape(tokens_here, width)
     columns = normed
-    result = jnp.dot(
-        columns,
-        lax.all_gather(w_out, "ctx", axis=0, tiled=True),
-        preferred_element_type=jnp.float32,
-    )
+    result = jnp.dot(columns, _review_core(w_out), preferred_element_type=jnp.float32)
     return result.astype(jnp.bfloat16)
 
 

time: 180 us -> 163 us (0.906)
  waiting for transfers between devices: 133 us -> 77.4 us
  starting transfers between devices: 0.08 us -> 30.2 us
  local copies, waits for them, and re-layouts: 0.09 us -> 3.26 us
  matrix products: 18.3 us -> 20.6 us
  other arithmetic: 14.6 us -> 16.5 us
    all_gather x1, waiting for transfers between devices: 66.9 us -> 29.5 us  [local(): lax.all_gather(w_qkv, 'ctx', axis=0, tiled=True)]
    ppermute x0 -> x15, waiting for transfers between devices: none -> 30.8 us  [the longest x8 16 us: _review_core(): next_value = lax.ppermute(next_value, 'ctx', vec_out)]
    ppermute x0 -> x15, starting transfers between devices: none -> 30.1 us  [the longest x7 30.1 us: _review_core(): clean = lax.ppermute(clean, 'ctx', met_up)]
    all_gather x1 -> x0, waiting for transfers between devices: 25.4 us -> none  [local(): lax.all_gather(w_out, 'ctx', axis=0, tiled=True)]
    all_gather x1, waiting for transfers between devices: 39.2 us -> 16.4 us  [carried_in(): pieces = lax.all_gather(value, axis)]
    dynamic_update_slice x0 -> x16, local copies, waits for them, and re-layouts: none -> 2.95 us  [the longest x8 1.91 us: _review_core(): lax.dynamic_update_slice_in_dim(local_now, next_value, (now - ii) % g_now...]
    dot_general x1, matrix products: 1.63 us -> 3.81 us  [local(): jnp.einsum('hts,she->the', scores, values, preferred_element_type=jnp.flo...]
  transfers between devices with their start and end apart: 3 -> 17, of which waited for: 3 -> 12; matrix products, arithmetic and copies ran while one was open for 9% -> 9% of each run, Pallas kernels for 0% -> 0%
where the time goes in v1:
time: 163 us; the launch traced here: 162 us
  waiting for transfers between devices  77.4 us (47%)
  starting transfers between devices  30.2 us (19%)
  matrix products  20.6 us (13%)
  other arithmetic  16.5 us (10%)
  between operations  13.8 us (8%)
  local copies, waits for them, and re-layouts  3.26 us (2%)
    ppermute x7, starting transfers between devices, _review_core(): clean = lax.ppermute(clean, 'ctx', met_up)  30.1 us
    all_gather x1, waiting for transfers between devices, local(): lax.all_gather(w_qkv, 'ctx', axis=0, tiled=True)  29.5 us
    all_gather x1, waiting for transfers between devices, carried_in(): pieces = lax.all_gather(value, axis)  16.4 us
    ppermute x8, waiting for transfers between devices, _review_core(): next_value = lax.ppermute(next_value, 'ctx', vec_out)  16 us
    ppermute x7, waiting for transfers between devices, _review_core(): clean = lax.ppermute(clean, 'ctx', met_up)  14.8 us
    select_n x15, other arithmetic, turn(): return jnp.where(position < mine, longer, running)  14.2 us
    dot_general x1, matrix products, local(): jnp.dot(columns, lax.all_gather(w_qkv, 'ctx', axis=0, tiled=True), prefer...  9.06 us
    dot_general x1, matrix products, local(): jnp.dot(columns, _review_core(w_out), preferred_element_type=jnp.float32)  4.55 us
  transfers between devices with their start and end apart: 17, of which 12 were waited for; matrix products, arithmetic and copies ran while one was open for 9% of the time, Pallas kernels for 0%

profile of v1, /device:TPU:0, one launch (start us, length us, event | category | flops | bytes accessed | tf_op | source)
XLA Modules:
  0.0 162.1 jit_solution(17767712583549779066)
XLA Ops:
  6.5 0.0 all-gather.4.cloned.1.call-start
  6.5 0.7 all-gather.4.cloned.1.call-update
  7.3 0.0 all-gather.6.cloned.1.call-start
  7.3 5.5 %collective-permute-start.1 = (bf16[16,4096]{1,0:T(8,128)(2,1)}, bf16[16,4096]{1,0:T(8,128)(2,1)S(1)}, u32[]{:S(2)}, u32[]{:S(2)}) collective-permute-start(bf16[16,4096]{1,0:T(8,128)(2,1)} %param.9), channel_id=1, source_target_pairs={{0,15},{1,0},{2,1},{3,2},{4,3},{5,4},{6,5},{7,6},{8,7},{9,8},{10,9... | collective-permute-start | bytes 393224 | tf_op jit(solution)/shard_map/ppermute | solution.py:24
  12.8 0.0 collective-permute-start
  12.8 0.2 broadcast_in_dim.25
  13.3 1.0 iota_compare_fusion
  14.3 1.4 collective-permute-done.1
  15.6 4.5 %collective-permute-start.3 = (bf16[16,4096]{1,0:T(8,128)(2,1)S(1)}, bf16[16,4096]{1,0:T(8,128)(2,1)S(1)}, u32[]{:S(2)}, u32[]{:S(2)}) collective-permute-start(bf16[16,4096]{1,0:T(8,128)(2,1)S(1)} %collective-permute-done.1), channel_id=1, source_target_pairs={{0,15},{1,0},{2,1},{3,2},{4,3},{5,4},{6,5},{7,6},{8,7},{9,8},{10,9... | collective-permute-start | bytes 393224 | tf_op jit(solution)/shard_map/ppermute | solution.py:24
  20.1 0.0 collective-permute-done
  20.1 0.0 collective-permute-start.2
  20.1 5.2 %collective-permute-done.3 = bf16[16,4096]{1,0:T(8,128)(2,1)S(1)} collective-permute-done((bf16[16,4096]{1,0:T(8,128)(2,1)S(1)}, bf16[16,4096]{1,0:T(8,128)(2,1)S(1)}, u32[]{:S(2)}, u32[]{:S(2)}) %collective-permute-start.3) | collective-permute-done | bytes 131104 | tf_op jit(solution)/shard_map/ppermute | solution.py:24
  25.3 4.6 %collective-permute-start.5 = (bf16[16,4096]{1,0:T(8,128)(2,1)S(1)}, bf16[16,4096]{1,0:T(8,128)(2,1)S(1)}, u32[]{:S(2)}, u32[]{:S(2)}) collective-permute-start(bf16[16,4096]{1,0:T(8,128)(2,1)S(1)} %collective-permute-done.3), channel_id=1, source_target_pairs={{0,15},{1,0},{2,1},{3,2},{4,3},{5,4},{6,5},{7,6},{8,7},{9,8},{10,9... | collective-permute-start | bytes 393224 | tf_op jit(solution)/shard_map/ppermute | solution.py:24
  30.0 0.0 collective-permute-done.2
  30.0 0.0 collective-permute-start.4
  30.0 5.0 %collective-permute-done.5 = bf16[16,4096]{1,0:T(8,128)(2,1)S(1)} collective-permute-done((bf16[16,4096]{1,0:T(8,128)(2,1)S(1)}, bf16[16,4096]{1,0:T(8,128)(2,1)S(1)}, u32[]{:S(2)}, u32[]{:S(2)}) %collective-permute-start.5) | collective-permute-done | bytes 131104 | tf_op jit(solution)/shard_map/ppermute | solution.py:24
  35.0 4.6 %collective-permute-start.7 = (bf16[16,4096]{1,0:T(8,128)(2,1)S(1)}, bf16[16,4096]{1,0:T(8,128)(2,1)S(1)}, u32[]{:S(2)}, u32[]{:S(2)}) collective-permute-start(bf16[16,4096]{1,0:T(8,128)(2,1)S(1)} %collective-permute-done.5), channel_id=1, source_target_pairs={{0,15},{1,0},{2,1},{3,2},{4,3},{5,4},{6,5},{7,6},{8,7},{9,8},{10,9... | collective-permute-start | bytes 393224 | tf_op jit(solution)/shard_map/ppermute | solution.py:24
  39.6 0.2 collective-permute-done.4
  39.9 0.0 collective-permute-start.6
  39.9 2.2 %collective-permute-done.7 = bf16[16,4096]{1,0:T(8,128)(2,1)S(1)} collective-permute-done((bf16[16,4096]{1,0:T(8,128)(2,1)S(1)}, bf16[16,4096]{1,0:T(8,128)(2,1)S(1)}, u32[]{:S(2)}, u32[]{:S(2)}) %collective-permute-start.7) | collective-permute-done | bytes 131104 | tf_op jit(solution)/shard_map/ppermute | solution.py:24
  42.1 4.6 %collective-permute-start.9 = (bf16[16,4096]{1,0:T(8,128)(2,1)S(1)}, bf16[16,4096]{1,0:T(8,128)(2,1)}, u32[]{:S(2)}, u32[]{:S(2)}) collective-permute-start(bf16[16,4096]{1,0:T(8,128)(2,1)S(1)} %collective-permute-done.7), channel_id=1, source_target_pairs={{0,15},{1,0},{2,1},{3,2},{4,3},{5,4},{6,5},{7,6},{8,7},{9,8},{10,9... | collective-permute-start | bytes 393224 | tf_op jit(solution)/shard_map/ppermute | solution.py:24
  46.7 0.4 collective-permute-done.6
  47.1 0.0 collective-permute-start.8
  47.1 29.5 %all-gather.4.cloned.1.call-done = bf16[4096,768]{1,0:T(8,128)(2,1)} async-done(((bf16[256,768]{1,0:T(8,128)(2,1)}), bf16[4096,768]{1,0:T(8,128)(2,1)}) %all-gather.4.cloned.1.call-update) | async-done | bytes 6291472 | tf_op jit(solution)/shard_map/all_gather | solution.py:52
  76.6 9.1 %convolution_convert_fusion.1 = bf16[768,768]{0,1:T(8,128)(2,1)S(1)} fusion(bf16[768,4096]{1,0:T(8,128)(2,1)} %param.7, bf16[4096,768]{1,0:T(8,128)(2,1)} %all-gather.4.cloned.1.call-done), kind=kOutput, calls=%fused_computation.8 | convolution fusion | flops 4832428032 | bytes 13762560 | tf_op jit(solution)/shard_map/dot_general | solution.py:50
  85.7 0.1 fusion.10
  85.8 0.9 fusion.11
  86.7 0.0 all-gather.6.cloned.1.call-update
  86.7 0.9 constant_dynamic-update-slice_fusion.8
  87.7 0.0 collective-permute-done.9
  87.7 1.9 %collective-permute-start.11 = (bf16[16,4096]{1,0:T(8,128)(2,1)}, bf16[16,4096]{1,0:T(8,128)(2,1)S(1)}, u32[]{:S(2)}, u32[]{:S(2)}) collective-permute-start(bf16[16,4096]{1,0:T(8,128)(2,1)} %collective-permute-done.9), channel_id=1, source_target_pairs={{0,15},{1,0},{2,1},{3,2},{4,3},{5,4},{6,5},{7,6},{8,7},{9,8},{10,9... | collective-permute-start | bytes 393224 | tf_op jit(solution)/shard_map/ppermute | solution.py:24
  89.6 0.0 collective-permute-done.8
  89.6 0.0 collective-permute-start.10
  89.6 0.9 constant_dynamic-update-slice_fusion.6
  90.5 0.9 constant_dynamic-update-slice_fusion.5
  91.4 1.0 collective-permute-done.11
  92.4 4.5 %collective-permute-start.13 = (bf16[16,4096]{1,0:T(8,128)(2,1)S(1)}, bf16[16,4096]{1,0:T(8,128)(2,1)S(1)}, u32[]{:S(2)}, u32[]{:S(2)}) collective-permute-start(bf16[16,4096]{1,0:T(8,128)(2,1)S(1)} %collective-permute-done.11), channel_id=1, source_target_pairs={{0,15},{1,0},{2,1},{3,2},{4,3},{5,4},{6,5},{7,6},{8,7},{9,8},{10,9... | collective-permute-start | bytes 393224 | tf_op jit(solution)/shard_map/ppermute | solution.py:24
  96.9 0.1 collective-permute-done.10
  97.0 0.0 collective-permute-start.12
  97.0 8.2 %collective-permute-done.12 = bf16[16,4096]{1,0:T(8,128)(2,1)S(1)} collective-permute-done((bf16[16,4096]{1,0:T(8,128)(2,1)S(1)}, bf16[16,4096]{1,0:T(8,128)(2,1)S(1)}, u32[]{:S(2)}, u32[]{:S(2)}) %collective-permute-start.12) | collective-permute-done | bytes 131104 | tf_op jit(solution)/shard_map/ppermute | solution.py:18
  105.3 0.0 collective-permute-start.14
  105.3 0.0 collective-permute-done.13
  105.3 7.0 %collective-permute-done.14 = bf16[16,4096]{1,0:T(8,128)(2,1)S(1)} collective-permute-done((bf16[16,4096]{1,0:T(8,128)(2,1)S(1)}, bf16[16,4096]{1,0:T(8,128)(2,1)S(1)}, u32[]{:S(2)}, u32[]{:S(2)}) %collective-permute-start.14) | collective-permute-done | bytes 131104 | tf_op jit(solution)/shard_map/ppermute | solution.py:18
  112.4 16.4 %all-gather.6.cloned.1.call-done = f32[32,128,128]{2,1,0:T(8,128)} async-done(((f32[2,128,128]{2,1,0:T(8,128)}), f32[32,128,128]{2,1,0:T(8,128)}) %all-gather.6.cloned.1.call-update) | async-done | bytes 2097168 | tf_op jit(solution)/shard_map/all_gather | solution.py:34
  128.8 14.6 %while.14 = (s32[]{:T(128)}, f32[2,128,128]{2,1,0:T(8,128)S(1)}, s32[]{:T(128)}, f32[16,2,128,128]{3,2,1,0:T(8,128)}, s32[]{:T(128)}, /*index=5*/s32[]{:T(128)}) while((s32[]{:T(128)}, f32[2,128,128]{2,1,0:T(8,128)S(1)}, s32[]{:T(128)}, f32[16,2,128,128]{3,2,1,0:T(8,128)}, s32[]{:T(128)}, /*index=5*/s32[]{:T(128)}) %tuple.42), condition=%wide.region_1.2_spmd.clone, body=%wide.region_0.1_spmd.clone.sunk | while | flops 98308 | bytes 393317 | solution.py:41
  128.8 0.9 add_select_fusion.2
  129.7 0.9 add_select_fusion.2
  130.7 0.9 add_select_fusion.2
  131.7 0.9 add_select_fusion.2
  132.6 0.9 add_select_fusion.2
  133.6 0.9 add_select_fusion.2
  134.6 0.9 add_select_fusion.2
  135.6 0.9 add_select_fusion.2
  136.5 0.9 add_select_fusion.2
  137.5 0.9 add_select_fusion.2
  138.5 0.9 add_select_fusion.2
  139.5 0.9 add_select_fusion.2
  140.4 0.9 add_select_fusion.2
  141.4 0.9 add_select_fusion.2
  142.4 0.9 add_select_fusion.2
  143.3 2.3 %fusion.7 = f32[2,128,768]{2,1,0:T(8,128)} fusion(bf16[768,2,128]{0,2,1:T(8,128)(2,1)S(1)} %bitcast.27, f32[2,128,128]{2,1,0:T(8,128)} %param.11, f32[2,128,128]{2,1,0:T(8,128)S(1)} %get-tuple-element.84), kind=kOutput, calls=%fused_computation.13 | convolution fusion | flops 302022656 | bytes 1441792 | tf_op jit(solution)/shard_map/thd,hde->the/dot_general | solution.py:71
  145.6 3.8 %multiply_reduce_fusion = (f32[768,2]{0,1:T(2,128)S(1)}, f32[768,2,128]{0,2,1:T(8,128)}) fusion(f32[2,128,768]{2,1,0:T(8,128)} %fusion.7, bf16[768,2,128]{0,2,1:T(8,128)(2,1)S(1)} %bitcast.24, bf16[768,2,128]{0,2,1:T(8,128)(2,1)S(1)} %bitcast.28, bf16[768,2,128]{0,2,1:T(8,128)(2,1)S(1)} %bitcast.26, pred[768,768]{1,0:T(8,128)(4,1)} %iota_compare_fusion), kind=kOutput, calls=%fused_computation.12 | convolution fusion | flops 606927360 | bytes 3348480 | tf_op jit(solution)/shard_map/hts,she->the/dot_general | solution.py:70
  149.5 1.2 multiply_convert_fusion
  150.7 4.5 %convolution_convert_fusion = bf16[768,4096]{1,0:T(8,128)(2,1)} fusion(bf16[768,256]{0,1:T(8,128)(2,1)S(1)} %bitcast.22, bf16[256,4096]{1,0:T(8,128)(2,1)S(1)} %constant_dynamic-update-slice_fusion), kind=kOutput, calls=%fused_computation.1 | convolution fusion | flops 1613758464 | bytes 8781824 | tf_op jit(solution)/shard_map/dot_general | solution.py:79
  (19 shorter events, 0.2 us)
Async XLA Ops:
  6.5 6.5 %copy-start = (bf16[16,4096]{1,0:T(8,128)(2,1)S(1)}, bf16[16,4096]{1,0:T(8,128)(2,1)}, u32[]{:S(2)}) copy-start(bf16[16,4096]{1,0:T(8,128)(2,1)} %param.9) | copy-start | bytes 393220
  6.5 70.1 %all-gather.4.cloned.1.call-start = ((), (), s32[]{:S(2)}) async-start(), calls=%async_computation | async-start | bytes 6684672 | tf_op jit(solution)/shard_map/all_gather | solution.py:52
  7.3 121.5 %all-gather.6.cloned.1.call-start = ((), (), s32[]{:S(2)}) async-start(), calls=%async_computation.1 | async-start | bytes 2228224 | tf_op jit(solution)/shard_map/all_gather | solution.py:34
  7.3 8.3 %collective-permute-start.1 = (bf16[16,4096]{1,0:T(8,128)(2,1)}, bf16[16,4096]{1,0:T(8,128)(2,1)S(1)}, u32[]{:S(2)}, u32[]{:S(2)}) collective-permute-start(bf16[16,4096]{1,0:T(8,128)(2,1)} %param.9), channel_id=1, source_target_pairs={{0,15},{1,0},{2,1},{3,2},{4,3},{5,4},{6,5},{7,6},{8,7},{9,8},{10,9... | collective-permute-start | bytes 393224 | tf_op jit(solution)/shard_map/ppermute | solution.py:24
  12.8 7.3 %collective-permute-start = (bf16[16,4096]{1,0:T(8,128)(2,1)}, bf16[16,4096]{1,0:T(8,128)(2,1)S(1)}, u32[]{:S(2)}, u32[]{:S(2)}) collective-permute-start(bf16[16,4096]{1,0:T(8,128)(2,1)} %param.9), channel_id=1, source_target_pairs={{0,1},{1,2},{2,3},{3,4},{4,5},{5,6},{6,7},{7,8},{8,9},{9,10},{10,1... | collective-permute-start | bytes 393224 | tf_op jit(solution)/shard_map/ppermute | solution.py:18
  15.6 9.7 %collective-permute-start.3 = (bf16[16,4096]{1,0:T(8,128)(2,1)S(1)}, bf16[16,4096]{1,0:T(8,128)(2,1)S(1)}, u32[]{:S(2)}, u32[]{:S(2)}) collective-permute-start(bf16[16,4096]{1,0:T(8,128)(2,1)S(1)} %collective-permute-done.1), channel_id=1, source_target_pairs={{0,15},{1,0},{2,1},{3,2},{4,3},{5,4},{6,5},{7,6},{8,7},{9,8},{10,9... | collective-permute-start | bytes 393224 | tf_op jit(solution)/shard_map/ppermute | solution.py:24
  20.1 9.9 %collective-permute-start.2 = (bf16[16,4096]{1,0:T(8,128)(2,1)S(1)}, bf16[16,4096]{1,0:T(8,128)(2,1)S(1)}, u32[]{:S(2)}, u32[]{:S(2)}) collective-permute-start(bf16[16,4096]{1,0:T(8,128)(2,1)S(1)} %collective-permute-done), channel_id=1, source_target_pairs={{0,1},{1,2},{2,3},{3,4},{4,5},{5,6},{6,7},{7,8},{8,9},{9,10},{10,1... | collective-permute-start | bytes 393224 | tf_op jit(solution)/shard_map/ppermute | solution.py:18
  25.3 9.7 %collective-permute-start.5 = (bf16[16,4096]{1,0:T(8,128)(2,1)S(1)}, bf16[16,4096]{1,0:T(8,128)(2,1)S(1)}, u32[]{:S(2)}, u32[]{:S(2)}) collective-permute-start(bf16[16,4096]{1,0:T(8,128)(2,1)S(1)} %collective-permute-done.3), channel_id=1, source_target_pairs={{0,15},{1,0},{2,1},{3,2},{4,3},{5,4},{6,5},{7,6},{8,7},{9,8},{10,9... | collective-permute-start | bytes 393224 | tf_op jit(solution)/shard_map/ppermute | solution.py:24
  30.0 9.9 %collective-permute-start.4 = (bf16[16,4096]{1,0:T(8,128)(2,1)S(1)}, bf16[16,4096]{1,0:T(8,128)(2,1)S(1)}, u32[]{:S(2)}, u32[]{:S(2)}) collective-permute-start(bf16[16,4096]{1,0:T(8,128)(2,1)S(1)} %collective-permute-done.2), channel_id=1, source_target_pairs={{0,1},{1,2},{2,3},{3,4},{4,5},{5,6},{6,7},{7,8},{8,9},{9,10},{10,1... | collective-permute-start | bytes 393224 | tf_op jit(solution)/shard_map/ppermute | solution.py:18
  35.0 7.1 %collective-permute-start.7 = (bf16[16,4096]{1,0:T(8,128)(2,1)S(1)}, bf16[16,4096]{1,0:T(8,128)(2,1)S(1)}, u32[]{:S(2)}, u32[]{:S(2)}) collective-permute-start(bf16[16,4096]{1,0:T(8,128)(2,1)S(1)} %collective-permute-done.5), channel_id=1, source_target_pairs={{0,15},{1,0},{2,1},{3,2},{4,3},{5,4},{6,5},{7,6},{8,7},{9,8},{10,9... | collective-permute-start | bytes 393224 | tf_op jit(solution)/shard_map/ppermute | solution.py:24
  39.9 7.3 %collective-permute-start.6 = (bf16[16,4096]{1,0:T(8,128)(2,1)S(1)}, bf16[16,4096]{1,0:T(8,128)(2,1)}, u32[]{:S(2)}, u32[]{:S(2)}) collective-permute-start(bf16[16,4096]{1,0:T(8,128)(2,1)S(1)} %collective-permute-done.4), channel_id=1, source_target_pairs={{0,1},{1,2},{2,3},{3,4},{4,5},{5,6},{6,7},{7,8},{8,9},{9,10},{10,1... | collective-permute-start | bytes 393224 | tf_op jit(solution)/shard_map/ppermute | solution.py:18
  42.1 45.5 %collective-permute-start.9 = (bf16[16,4096]{1,0:T(8,128)(2,1)S(1)}, bf16[16,4096]{1,0:T(8,128)(2,1)}, u32[]{:S(2)}, u32[]{:S(2)}) collective-permute-start(bf16[16,4096]{1,0:T(8,128)(2,1)S(1)} %collective-permute-done.7), channel_id=1, source_target_pairs={{0,15},{1,0},{2,1},{3,2},{4,3},{5,4},{6,5},{7,6},{8,7},{9,8},{10,9... | collective-permute-start | bytes 393224 | tf_op jit(solution)/shard_map/ppermute | solution.py:24
  47.1 42.5 %collective-permute-start.8 = (bf16[16,4096]{1,0:T(8,128)(2,1)}, bf16[16,4096]{1,0:T(8,128)(2,1)}, u32[]{:S(2)}, u32[]{:S(2)}) collective-permute-start(bf16[16,4096]{1,0:T(8,128)(2,1)} %collective-permute-done.6), channel_id=1, source_target_pairs={{0,1},{1,2},{2,3},{3,4},{4,5},{5,6},{6,7},{7,8},{8,9},{9,10},{10,1... | collective-permute-start | bytes 393224 | tf_op jit(solution)/shard_map/ppermute | solution.py:18
  87.7 4.7 %collective-permute-start.11 = (bf16[16,4096]{1,0:T(8,128)(2,1)}, bf16[16,4096]{1,0:T(8,128)(2,1)S(1)}, u32[]{:S(2)}, u32[]{:S(2)}) collective-permute-start(bf16[16,4096]{1,0:T(8,128)(2,1)} %collective-permute-done.9), channel_id=1, source_target_pairs={{0,15},{1,0},{2,1},{3,2},{4,3},{5,4},{6,5},{7,6},{8,7},{9,8},{10,9... | collective-permute-start | bytes 393224 | tf_op jit(solution)/shard_map/ppermute | solution.py:24
  89.6 7.4 %collective-permute-start.10 = (bf16[16,4096]{1,0:T(8,128)(2,1)}, bf16[16,4096]{1,0:T(8,128)(2,1)S(1)}, u32[]{:S(2)}, u32[]{:S(2)}) collective-permute-start(bf16[16,4096]{1,0:T(8,128)(2,1)} %collective-permute-done.8), channel_id=1, source_target_pairs={{0,1},{1,2},{2,3},{3,4},{4,5},{5,6},{6,7},{7,8},{8,9},{9,10},{10,1... | collective-permute-start | bytes 393224 | tf_op jit(solution)/shard_map/ppermute | solution.py:18
  92.4 12.9 %collective-permute-start.13 = (bf16[16,4096]{1,0:T(8,128)(2,1)S(1)}, bf16[16,4096]{1,0:T(8,128)(2,1)S(1)}, u32[]{:S(2)}, u32[]{:S(2)}) collective-permute-start(bf16[16,4096]{1,0:T(8,128)(2,1)S(1)} %collective-permute-done.11), channel_id=1, source_target_pairs={{0,15},{1,0},{2,1},{3,2},{4,3},{5,4},{6,5},{7,6},{8,7},{9,8},{10,9... | collective-permute-start | bytes 393224 | tf_op jit(solution)/shard_map/ppermute | solution.py:24
  97.0 8.3 %collective-permute-start.12 = (bf16[16,4096]{1,0:T(8,128)(2,1)S(1)}, bf16[16,4096]{1,0:T(8,128)(2,1)S(1)}, u32[]{:S(2)}, u32[]{:S(2)}) collective-permute-start(bf16[16,4096]{1,0:T(8,128)(2,1)S(1)} %collective-permute-done.10), channel_id=1, source_target_pairs={{0,1},{1,2},{2,3},{3,4},{4,5},{5,6},{6,7},{7,8},{8,9},{9,10},{10,1... | collective-permute-start | bytes 393224 | tf_op jit(solution)/shard_map/ppermute | solution.py:18
  105.3 7.1 %collective-permute-start.14 = (bf16[16,4096]{1,0:T(8,128)(2,1)S(1)}, bf16[16,4096]{1,0:T(8,128)(2,1)S(1)}, u32[]{:S(2)}, u32[]{:S(2)}) collective-permute-start(bf16[16,4096]{1,0:T(8,128)(2,1)S(1)} %collective-permute-done.12), channel_id=1, source_target_pairs={{0,1},{1,2},{2,3},{3,4},{4,5},{5,6},{6,7},{7,8},{8,9},{9,10},{10,1... | collective-permute-start | bytes 393224 | tf_op jit(solution)/shard_map/ppermute | solution.py:18
  145.6 3.8 %copy-start.1 = (f32[256]{0:T(256)S(1)}, f32[256]{0:T(256)}, u32[]{:S(2)}) copy-start(f32[256]{0:T(256)} %param.10) | copy-start | bytes 3076
Sparse Core Ops, SparseCore 0:
  9.6 66.9 all-gather.3
  86.8 41.8 all-gather.5
